TPU v7x, 256 devices: a whole 4x4x8 slice. The times are simulated.
256 devices in a mesh: row: 16 (over y_hi, x, core), col: 8 (over z), rep: 2 (over y_lo).
Axes of the slice: x: 4, y: 4 (y_hi: 2, y_lo: 2; y = y_hi * 2 + y_lo), z: 8, core: 2. Of those that a mesh axis runs over, the one named last changes fastest.
Arguments:
- features: bfloat16 [32768, 512], P(('row', 'col', 'rep')), may hold values from -6 to 6
- tile_values: bfloat16 [32768, 128, 128], P(('row', 'col', 'rep')), as said below
- tile_coords: int32 [32768, 2], P(('row', 'col', 'rep')), may hold values from 0 to 15, as said below
- tile_counts: int32 [256], P(('row', 'col', 'rep')), may hold values from 16 to 128, as said below
- weight: bfloat16 [512, 512], replicated, may hold values from -0.25 to 0.25
- cotangent: bfloat16 [32768, 512], P(('row', 'col', 'rep')), may hold values from -6 to 6
Outputs:
- activations: bfloat16 [32768, 512], P(('row', 'col', 'rep'))
- grad_features: bfloat16 [32768, 512], P(('row', 'col', 'rep'))
- grad_weight: float32 [512, 512], replicated
Inputs may be any that keep to these rules, and one draw needn't show every extreme that they name: `tile_values`: nonnegative edge weights; slots past a block's live count hold values that must be ignored. `tile_coords`: column 0 is a tile row below 16, column 1 a tile column below 16; within one block no tile position appears twice. `tile_counts`: live slots differ from block to block; some block uses all 128 slots.
All inputs are finite; a program needn't handle non-finite values.
Results may differ from a plain program's by a relative error of at most 0.028.
Values may be sent and summed in bfloat16 or wider, within the bound.
No kernel may reach another device: no remote copies, remote signals or barrier semaphores. Data moves between devices by JAX's collectives and lax.ppermute only.
A program may use at most 128 MiB of HBM per device.

v0:
```python
import math

import jax
import jax.numpy as jnp
from jax import lax
from jax.sharding import PartitionSpec as P


def silu_slope(values_in):
    sigmoid_v = jax.nn.sigmoid(values_in)
    return sigmoid_v * (1.0 + values_in * (1.0 - sigmoid_v))


def tile_product(tile_values, tile_coords, live_mask, source, out_tiles, transposed):
    slot_count, tile_size, _ = tile_values.shape
    feat_width = source.shape[-1]
    bunch_size = math.gcd(slot_count, 32)

    def one_bunch(counter, running):
        offset = counter * bunch_size
        tile_block = lax.dynamic_slice_in_dim(tile_values, offset, bunch_size, 0)
        coord_block = lax.dynamic_slice_in_dim(tile_coords, offset, bunch_size, 0)
        live_block = lax.dynamic_slice_in_dim(live_mask, offset, bunch_size, 0)
        if transposed:
            picked = source[coord_block[:, 0]]
            products = jnp.einsum(
                "kji,kjf->kif", tile_block, picked, preferred_element_type=jnp.float32
            )
            target = coord_block[:, 1]
        else:
            picked = source[coord_block[:, 1]]
            products = jnp.einsum(
                "kij,kjf->kif", tile_block, picked, preferred_element_type=jnp.float32
            )
            target = coord_block[:, 0]
        return running.at[target].add(products * live_block[:, None, None])

    zero_tiles = jnp.zeros((out_tiles, tile_size, feat_width), jnp.float32)
    running = lax.fori_loop(0, slot_count // bunch_size, one_bunch, zero_tiles)
    return running.reshape(out_tiles * tile_size, feat_width).astype(jnp.bfloat16)


def sum_weights(weight_local):
    return lax.psum(weight_local, ("row", "col", "rep"))


def body(features, tile_values, tile_coords, tile_counts, weight, cotangent):
    rows_dev = features.shape[0]
    tile_size = tile_values.shape[1]
    feat_width = features.shape[1]
    slot_count = tile_values.shape[0]
    col_groups = lax.axis_size(("col", "rep"))
    row_groups = lax.axis_size("row")
    live_mask = (jnp.arange(slot_count) < tile_counts[0]).astype(jnp.float32)
    contract_last = (((1,), (1,)), ((), ()))
    contract_first = (((0,), (0,)), ((), ()))
    panel_rows = lax.all_gather(features, "row", axis=0, tiled=True)
    source_tiles = panel_rows.reshape(-1, tile_size, feat_width)
    partial_rows = tile_product(
        tile_values, tile_coords, live_mask, source_tiles, col_groups * rows_dev // tile_size, False
    )
    summed = lax.psum_scatter(partial_rows, ("col", "rep"), scatter_dimension=0, tiled=True).astype(
        jnp.float32
    )
    aggregated = summed.astype(jnp.bfloat16)
    pre_act = jnp.dot(aggregated, weight, preferred_element_type=jnp.float32)
    pre_grad = (cotangent.astype(jnp.float32) * silu_slope(pre_act)).astype(jnp.bfloat16)
    own_grad = lax.dot_general(
        pre_grad, weight, contract_last, preferred_element_type=jnp.float32
    ).astype(jnp.bfloat16)
    row_grad = lax.all_gather(own_grad, ("col", "rep"), axis=0, tiled=True)
    activations = jax.nn.silu(pre_act).astype(jnp.bfloat16)
    weight_local = lax.dot_general(
        aggregated, pre_grad, contract_first, preferred_element_type=jnp.float32
    )
    norm_factor = lax.rsqrt(jnp.float32(rows_dev * row_groups * col_groups))
    grad_tiles = row_grad.reshape(-1, tile_size, feat_width)
    column_part = tile_product(
        tile_values, tile_coords, live_mask, grad_tiles, row_groups * rows_dev // tile_size, True
    )
    grad_weight = sum_weights(weight_local) * norm_factor
    grad_features = (
        lax.psum_scatter(column_part, "row", scatter_dimension=0, tiled=True)
        .astype(jnp.float32)
        .astype(jnp.bfloat16)
    )
    return (activations, grad_features, grad_weight)


def solution(mesh):
    placed = (
        P(("row", "col", "rep"), None),
        P(("row", "col", "rep"), None, None),
        P(("row", "col", "rep"), None),
        P(("row", "col", "rep")),
        P(),
        P(("row", "col", "rep"), None),
    )
    return jax.shard_map(
        body,
        mesh=mesh,
        in_specs=placed,
        out_specs=(P(("row", "col", "rep"), None), P(("row", "col", "rep"), None), P()),
        check_vma=False,
    )
```

profile of v0, /device:TPU:1, one launch (start us, length us, event | category | flops | bytes accessed | tf_op | source)
XLA Modules:
  0.0 684.3 jit_solution(8421702360190963024)
XLA Ops:
  7.2 0.0 all-gather.3.cloned.1.call-start
  7.2 0.7 all-gather.3.cloned.1.call-update
  7.9 0.0 reduce-scatter.3.cloned.1.call-start
  8.6 59.9 %all-gather.3.cloned.1.call-done = bf16[2048,512]{1,0:T(8,128)(2,1)} async-done(((bf16[128,512]{1,0:T(8,128)(2,1)}), bf16[2048,512]{1,0:T(8,128)(2,1)}) %all-gather.3.cloned.1.call-update) | async-done | bytes 2097168 | tf_op jit(solution)/shard_map/all_gather | solution.py:57
  68.5 2.5 broadcast.52.clone
  71.0 112.9 %while.26 = (s32[]{:T(128)}, f32[16,128,512]{2,1,0:T(8,128)}, s32[128,2]{0,1:T(2,128)S(1)}, bf16[128,128,128]{2,1,0:T(8,128)(2,1)}, bf16[16,128,512]{2,1,0:T(8,1...) while((s32[]{:T(128)}, f32[16,128,512]{2,1,0:T(8,128)}, ...), condition=%wide.region_2.0_spmd, body=%wide.region_0.0_spmd.sunk | while | flops 541066432 | bytes 47191976 | solution.py:39
  71.0 0.1 constant_dynamic-slice_fusion.4
  71.1 0.1 dynamic_slice.56
  71.2 2.7 gather_fusion
  73.9 7.0 %broadcast_multiply_fusion.5 = f32[32,128,512]{2,1,0:T(8,128)} fusion(f32[32]{0:T(128)S(1)} %dynamic_slice.56, bf16[32,128,512]{2,1,0:T(8,128)(2,1)} %gather_fusion, bf16[128,128,128]{2,1,0:T(8,128)(2,1)} %get-tuple-element.364, s32[]{:T(128)S(6)} %select_n.67), kind=kOutput, calls=%fused_computation.4.clone.1 | convolution fusion | flops 538968064 | bytes 13631620 | tf_op jit(solution)/shard_map/while/body/eval_jaxpr/kij,kjf->kif/dot_general | solution.py:32
  80.9 18.3 %scatter_fusion = f32[16,128,512]{2,1,0:T(8,128)} fusion(f32[16,128,512]{2,1,0:T(8,128)} %get-tuple-element.352, s32[32]{0:T(128)S(1)} %get-tuple-element.331, f32[32,128,512]{2,1,0:T(8,128)} %broadcast_multiply_fusion.5), kind=kCustom, calls=%fused_computation.2.clone.1 | custom fusion | flops 2097152 | bytes 25165952 | tf_op jit(solution)/shard_map/while/body/eval_jaxpr/scatter-add | solution.py:36
  99.2 0.1 constant_dynamic-slice_fusion.4
  99.3 0.1 dynamic_slice.56
  99.4 2.7 gather_fusion
  102.1 7.0 %broadcast_multiply_fusion.5 = f32[32,128,512]{2,1,0:T(8,128)} fusion(f32[32]{0:T(128)S(1)} %dynamic_slice.56, bf16[32,128,512]{2,1,0:T(8,128)(2,1)} %gather_fusion, bf16[128,128,128]{2,1,0:T(8,128)(2,1)} %get-tuple-element.364, s32[]{:T(128)S(6)} %select_n.67), kind=kOutput, calls=%fused_computation.4.clone.1 | convolution fusion | flops 538968064 | bytes 13631620 | tf_op jit(solution)/shard_map/while/body/eval_jaxpr/kij,kjf->kif/dot_general | solution.py:32
  109.1 18.6 %scatter_fusion = f32[16,128,512]{2,1,0:T(8,128)} fusion(f32[16,128,512]{2,1,0:T(8,128)} %get-tuple-element.352, s32[32]{0:T(128)S(1)} %get-tuple-element.331, f32[32,128,512]{2,1,0:T(8,128)} %broadcast_multiply_fusion.5), kind=kCustom, calls=%fused_computation.2.clone.1 | custom fusion | flops 2097152 | bytes 25165952 | tf_op jit(solution)/shard_map/while/body/eval_jaxpr/scatter-add | solution.py:36
  127.7 0.1 constant_dynamic-slice_fusion.4
  127.8 0.1 dynamic_slice.56
  127.8 2.7 gather_fusion
  130.6 7.0 %broadcast_multiply_fusion.5 = f32[32,128,512]{2,1,0:T(8,128)} fusion(f32[32]{0:T(128)S(1)} %dynamic_slice.56, bf16[32,128,512]{2,1,0:T(8,128)(2,1)} %gather_fusion, bf16[128,128,128]{2,1,0:T(8,128)(2,1)} %get-tuple-element.364, s32[]{:T(128)S(6)} %select_n.67), kind=kOutput, calls=%fused_computation.4.clone.1 | convolution fusion | flops 538968064 | bytes 13631620 | tf_op jit(solution)/shard_map/while/body/eval_jaxpr/kij,kjf->kif/dot_general | solution.py:32
  137.6 18.2 %scatter_fusion = f32[16,128,512]{2,1,0:T(8,128)} fusion(f32[16,128,512]{2,1,0:T(8,128)} %get-tuple-element.352, s32[32]{0:T(128)S(1)} %get-tuple-element.331, f32[32,128,512]{2,1,0:T(8,128)} %broadcast_multiply_fusion.5), kind=kCustom, calls=%fused_computation.2.clone.1 | custom fusion | flops 2097152 | bytes 25165952 | tf_op jit(solution)/shard_map/while/body/eval_jaxpr/scatter-add | solution.py:36
  155.8 0.1 constant_dynamic-slice_fusion.4
  155.8 0.1 dynamic_slice.56
  155.9 2.7 gather_fusion
  158.7 7.0 %broadcast_multiply_fusion.5 = f32[32,128,512]{2,1,0:T(8,128)} fusion(f32[32]{0:T(128)S(1)} %dynamic_slice.56, bf16[32,128,512]{2,1,0:T(8,128)(2,1)} %gather_fusion, bf16[128,128,128]{2,1,0:T(8,128)(2,1)} %get-tuple-element.364, s32[]{:T(128)S(6)} %select_n.67), kind=kOutput, calls=%fused_computation.4.clone.1 | convolution fusion | flops 538968064 | bytes 13631620 | tf_op jit(solution)/shard_map/while/body/eval_jaxpr/kij,kjf->kif/dot_general | solution.py:32
  165.6 18.2 %scatter_fusion = f32[16,128,512]{2,1,0:T(8,128)} fusion(f32[16,128,512]{2,1,0:T(8,128)} %get-tuple-element.352, s32[32]{0:T(128)S(1)} %get-tuple-element.331, f32[32,128,512]{2,1,0:T(8,128)} %broadcast_multiply_fusion.5), kind=kCustom, calls=%fused_computation.2.clone.1 | custom fusion | flops 2097152 | bytes 25165952 | tf_op jit(solution)/shard_map/while/body/eval_jaxpr/scatter-add | solution.py:36
  183.9 3.8 convert_element_type.32
  187.7 0.0 reduce-scatter.3.cloned.1.call-update
  187.8 0.0 all-gather.5.cloned.1.call-start
  187.8 63.4 %reduce-scatter.3.cloned.1.call-done = bf16[128,512]{1,0:T(8,128)(2,1)} async-done(((bf16[2048,512]{1,0:T(8,128)(2,1)}), bf16[128,512]{1,0:T(8,128)(2,1)}) %reduce-scatter.3.cloned.1.call-update) | async-done | bytes 131088 | tf_op jit(solution)/shard_map/reduce_scatter | solution.py:62
  251.2 1.8 multiply_convert_fusion.1
  253.0 1.0 convolution_convert_fusion
  254.0 0.0 all-gather.5.cloned.1.call-update
  254.0 0.0 all-reduce.2.cloned.1.call-start
  254.1 2.3 fusion.8
  256.3 0.0 reduce-scatter.5.cloned.1.call-start
  256.4 71.7 %all-gather.5.cloned.1.call-done = bf16[2048,512]{1,0:T(8,128)(2,1)} async-done(((bf16[128,512]{1,0:T(8,128)(2,1)}), bf16[2048,512]{1,0:T(8,128)(2,1)}) %all-gather.5.cloned.1.call-update) | async-done | bytes 2097168 | tf_op jit(solution)/shard_map/all_gather | solution.py:71
  328.0 2.5 broadcast.52
  330.5 114.6 %while.27 = (s32[]{:T(128)}, f32[16,128,512]{2,1,0:T(8,128)}, s32[128,2]{0,1:T(2,128)S(1)}, bf16[128,128,128]{2,1,0:T(8,128)(2,1)}, bf16[16,128,512]{2,1,0:T(8,1...) while((s32[]{:T(128)}, f32[16,128,512]{2,1,0:T(8,128)}, ...), condition=%wide.region_6.7_spmd, body=%wide.region_4.6_spmd.sunk | while | flops 541066432 | bytes 47191976 | solution.py:39
  330.5 0.1 constant_dynamic-slice_fusion.5
  330.6 0.1 dynamic_slice.59
  330.7 2.7 gather_fusion.1
  333.4 7.3 %broadcast_multiply_fusion.6 = f32[32,128,512]{2,1,0:T(8,128)} fusion(f32[32]{0:T(128)S(1)} %dynamic_slice.59, bf16[32,128,512]{2,1,0:T(8,128)(2,1)} %gather_fusion.1, bf16[128,128,128]{2,1,0:T(8,128)(2,1)} %get-tuple-element.394, s32[]{:T(128)S(6)} %select_n.69), kind=kOutput, calls=%fused_computation.13.clone.1 | convolution fusion | flops 538968064 | bytes 13631620 | tf_op jit(solution)/shard_map/while/body/eval_jaxpr/kji,kjf->kif/dot_general | solution.py:26
  340.7 18.5 %scatter_fusion.1 = f32[16,128,512]{2,1,0:T(8,128)} fusion(f32[16,128,512]{2,1,0:T(8,128)} %get-tuple-element.382, s32[32]{0:T(128)S(1)} %get-tuple-element.339, f32[32,128,512]{2,1,0:T(8,128)} %broadcast_multiply_fusion.6), kind=kCustom, calls=%fused_computation.3.clone.1 | custom fusion | flops 2097152 | bytes 25165952 | tf_op jit(solution)/shard_map/while/body/eval_jaxpr/scatter-add | solution.py:36
  359.2 0.1 constant_dynamic-slice_fusion.5
  359.3 0.1 dynamic_slice.59
  359.4 2.7 gather_fusion.1
  362.1 7.3 %broadcast_multiply_fusion.6 = f32[32,128,512]{2,1,0:T(8,128)} fusion(f32[32]{0:T(128)S(1)} %dynamic_slice.59, bf16[32,128,512]{2,1,0:T(8,128)(2,1)} %gather_fusion.1, bf16[128,128,128]{2,1,0:T(8,128)(2,1)} %get-tuple-element.394, s32[]{:T(128)S(6)} %select_n.69), kind=kOutput, calls=%fused_computation.13.clone.1 | convolution fusion | flops 538968064 | bytes 13631620 | tf_op jit(solution)/shard_map/while/body/eval_jaxpr/kji,kjf->kif/dot_general | solution.py:26
  369.4 18.7 %scatter_fusion.1 = f32[16,128,512]{2,1,0:T(8,128)} fusion(f32[16,128,512]{2,1,0:T(8,128)} %get-tuple-element.382, s32[32]{0:T(128)S(1)} %get-tuple-element.339, f32[32,128,512]{2,1,0:T(8,128)} %broadcast_multiply_fusion.6), kind=kCustom, calls=%fused_computation.3.clone.1 | custom fusion | flops 2097152 | bytes 25165952 | tf_op jit(solution)/shard_map/while/body/eval_jaxpr/scatter-add | solution.py:36
  388.1 0.1 constant_dynamic-slice_fusion.5
  388.1 0.1 dynamic_slice.59
  388.2 2.7 gather_fusion.1
  391.0 7.3 %broadcast_multiply_fusion.6 = f32[32,128,512]{2,1,0:T(8,128)} fusion(f32[32]{0:T(128)S(1)} %dynamic_slice.59, bf16[32,128,512]{2,1,0:T(8,128)(2,1)} %gather_fusion.1, bf16[128,128,128]{2,1,0:T(8,128)(2,1)} %get-tuple-element.394, s32[]{:T(128)S(6)} %select_n.69), kind=kOutput, calls=%fused_computation.13.clone.1 | convolution fusion | flops 538968064 | bytes 13631620 | tf_op jit(solution)/shard_map/while/body/eval_jaxpr/kji,kjf->kif/dot_general | solution.py:26
  398.2 18.3 %scatter_fusion.1 = f32[16,128,512]{2,1,0:T(8,128)} fusion(f32[16,128,512]{2,1,0:T(8,128)} %get-tuple-element.382, s32[32]{0:T(128)S(1)} %get-tuple-element.339, f32[32,128,512]{2,1,0:T(8,128)} %broadcast_multiply_fusion.6), kind=kCustom, calls=%fused_computation.3.clone.1 | custom fusion | flops 2097152 | bytes 25165952 | tf_op jit(solution)/shard_map/while/body/eval_jaxpr/scatter-add | solution.py:36
  416.6 0.1 constant_dynamic-slice_fusion.5
  416.6 0.1 dynamic_slice.59
  416.7 2.7 gather_fusion.1
  419.5 7.3 %broadcast_multiply_fusion.6 = f32[32,128,512]{2,1,0:T(8,128)} fusion(f32[32]{0:T(128)S(1)} %dynamic_slice.59, bf16[32,128,512]{2,1,0:T(8,128)(2,1)} %gather_fusion.1, bf16[128,128,128]{2,1,0:T(8,128)(2,1)} %get-tuple-element.394, s32[]{:T(128)S(6)} %select_n.69), kind=kOutput, calls=%fused_computation.13.clone.1 | convolution fusion | flops 538968064 | bytes 13631620 | tf_op jit(solution)/shard_map/while/body/eval_jaxpr/kji,kjf->kif/dot_general | solution.py:26
  426.7 18.4 %scatter_fusion.1 = f32[16,128,512]{2,1,0:T(8,128)} fusion(f32[16,128,512]{2,1,0:T(8,128)} %get-tuple-element.382, s32[32]{0:T(128)S(1)} %get-tuple-element.339, f32[32,128,512]{2,1,0:T(8,128)} %broadcast_multiply_fusion.6), kind=kCustom, calls=%fused_computation.3.clone.1 | custom fusion | flops 2097152 | bytes 25165952 | tf_op jit(solution)/shard_map/while/body/eval_jaxpr/scatter-add | solution.py:36
  445.1 3.8 convert_element_type.38
  448.9 0.0 reduce-scatter.5.cloned.1.call-update
  448.9 146.7 %all-reduce.2.cloned.1.call-done = f32[512,512]{1,0:T(8,128)} async-done(((f32[512,512]{1,0:T(8,128)}), f32[512,512]{1,0:T(8,128)}) %all-reduce.2.cloned.1.call-update) | async-done | bytes 1048592 | tf_op jit(solution)/shard_map/psum | solution.py:44
  595.6 2.3 broadcast_multiply_fusion.2
  597.9 79.8 %reduce-scatter.5.cloned.1.call-done = bf16[128,512]{1,0:T(8,128)(2,1)} async-done(((bf16[2048,512]{1,0:T(8,128)(2,1)}), bf16[128,512]{1,0:T(8,128)(2,1)}) %reduce-scatter.5.cloned.1.call-update) | async-done | bytes 131088 | tf_op jit(solution)/shard_map/reduce_scatter | solution.py:83
  (28 shorter events, 0.2 us)
Async XLA Ops:
  7.2 244.0 %copy-start = (bf16[512,512]{1,0:T(8,128)(2,1)S(1)}, bf16[512,512]{1,0:T(8,128)(2,1)}, u32[]{:S(2)}) copy-start(bf16[512,512]{1,0:T(8,128)(2,1)} %param.14) | copy-start | bytes 1572868
  7.2 63.8 %copy-start.3 = (s32[128,2]{0,1:T(2,128)S(1)}, s32[128,2]{0,1:T(2,128)}, u32[]{:S(2)}) copy-start(s32[128,2]{0,1:T(2,128)} %param.12) | copy-start | bytes 3076
  7.2 61.3 %all-gather.3.cloned.1.call-start = ((), (), s32[]{:S(2)}) async-start(), calls=%async_computation.2 | async-start | bytes 2228224 | tf_op jit(solution)/shard_map/all_gather | solution.py:57
  7.9 243.3 %reduce-scatter.3.cloned.1.call-start = ((), (), s32[]{:S(2)}) async-start(), calls=%async_computation.3 | async-start | bytes 2228224 | tf_op jit(solution)/shard_map/reduce_scatter | solution.py:62
  68.5 2.5 copy-start.2
  183.9 69.1 %copy-start.4 = (bf16[128,512]{1,0:T(8,128)(2,1)S(1)}, bf16[128,512]{1,0:T(8,128)(2,1)}, u32[]{:S(2)}) copy-start(bf16[128,512]{1,0:T(8,128)(2,1)} %param.15) | copy-start | bytes 393220
  187.8 140.3 %all-gather.5.cloned.1.call-start = ((), (), s32[]{:S(2)}) async-start(), calls=%async_computation.4 | async-start | bytes 2228224 | tf_op jit(solution)/shard_map/all_gather | solution.py:71
  254.0 341.6 %all-reduce.2.cloned.1.call-start = ((), (), s32[]{:S(2)}) async-start(), calls=%async_computation.6 | async-start | bytes 2097152 | tf_op jit(solution)/shard_map/psum | solution.py:44
  256.3 421.4 %reduce-scatter.5.cloned.1.call-start = ((), (), s32[]{:S(2)}) async-start(), calls=%async_computation.5 | async-start | bytes 2228224 | tf_op jit(solution)/shard_map/reduce_scatter | solution.py:83
  328.0 2.5 copy-start.1
Sparse Core Ops, SparseCore 0:
  10.8 57.6 all-gather.2
  187.9 63.2 reduce-scatter.2
  254.1 73.8 all-gather.4
  333.9 261.6 all-reduce.1
  600.9 76.8 reduce-scatter.4
where the time goes:
time: 686 us; the launch traced here: 684 us
  waiting for transfers between devices  422 us (62%)
  other arithmetic  157 us (23%)
  matrix products  62.1 us (9%)
  local copies, waits for them, and re-layouts  28.1 us (4%)
  between operations  14.5 us (2%)
    scatter-add x8, other arithmetic, one_bunch(): return running.at[target].add(products * live_block[:, None, None])  147 us
    psum x1, waiting for transfers between devices, sum_weights(): return lax.psum(weight_local, ('row', 'col', 'rep'))  147 us
    reduce_scatter x1, waiting for transfers between devices, body(): lax.psum_scatter(column_part, 'row', scatter_dimension=0, tiled=True)  79.8 us
    all_gather x1, waiting for transfers between devices, body(): row_grad = lax.all_gather(own_grad, ('col', 'rep'), axis=0, tiled=True)  71.7 us
    reduce_scatter x1, waiting for transfers between devices, body(): lax.psum_scatter(partial_rows, ('col', 'rep'), scatter_dimension=0, tiled...  63.4 us
    all_gather x1, waiting for transfers between devices, body(): panel_rows = lax.all_gather(features, 'row', axis=0, tiled=True)  59.9 us
    dot_general x4, matrix products, one_bunch(): jnp.einsum('kji,kjf->kif', tile_block, picked, preferred_element_type=jnp...  29.1 us
    dot_general x4, matrix products, one_bunch(): jnp.einsum('kij,kjf->kif', tile_block, picked, preferred_element_type=jnp...  27.9 us
  transfers between devices with their start and end apart: 5, of which 5 were waited for; matrix products, arithmetic and copies ran while one was open for 18% of the time, Pallas kernels for 0%

commit v1 on v0

v1 whole, which is shorter than its diff:
```python
import jax
import jax.numpy as jnp
from jax import lax
from jax.experimental import pallas as pl
from jax.experimental.pallas import tpu as pltpu
from jax.sharding import PartitionSpec as P

TILE = 128
BUNCH = 16
F32 = jnp.float32
BF16 = jnp.bfloat16
MIB = 1024 * 1024


def wide_sum(*terms):
    total = terms[0].astype(F32)
    for term in terms[1:]:
        total = total + term.astype(F32)
    return total.astype(BF16)


def dense_kernel(flip, counts_ref, places_ref, tiles_ref, dense_ref):
    step = pl.program_id(0)

    @pl.when(step == 0)
    def _():
        dense_ref[...] = jnp.zeros_like(dense_ref)

    def place(j, carry):
        slot = step * BUNCH + j

        @pl.when(slot < counts_ref[0])
        def _():
            top = pl.multiple_of(places_ref[2 * slot] * TILE, TILE)
            left = pl.multiple_of(places_ref[2 * slot + 1] * TILE, TILE)
            tile = tiles_ref[j]
            if flip:
                dense_ref[pl.ds(left, TILE), pl.ds(top, TILE)] = tile.T
            else:
                dense_ref[pl.ds(top, TILE), pl.ds(left, TILE)] = tile

        return carry

    lax.fori_loop(0, BUNCH, place, 0)


def dense_block(tile_values, places, tile_counts, side, flip):
    slots = tile_values.shape[0]
    return pl.pallas_call(
        lambda *refs: dense_kernel(flip, *refs),
        out_shape=jax.ShapeDtypeStruct((side, side), BF16),
        grid_spec=pltpu.PrefetchScalarGridSpec(
            num_scalar_prefetch=2,
            grid=(slots // BUNCH,),
            in_specs=[pl.BlockSpec((BUNCH, TILE, TILE), lambda g, *_: (g, 0, 0))],
            out_specs=pl.BlockSpec((side, side), lambda g, *_: (0, 0)),
        ),
        compiler_params=pltpu.CompilerParams(vmem_limit_bytes=28 * MIB),
        cost_estimate=pl.CostEstimate(flops=0, bytes_accessed=12 * MIB, transcendentals=0),
        name="flipped_build" if flip else "dense_build",
    )(tile_counts, places.reshape(-1), tile_values)


def pieces_dot_kernel(starts, dense_ref, *refs):
    out_ref = refs[-1]
    total = None
    for start, piece in zip(starts, refs[:-1]):
        depth = piece.shape[0]
        term = jnp.dot(
            dense_ref[:, start : start + depth], piece[...], preferred_element_type=F32
        )
        total = term if total is None else total + term
    out_ref[...] = total.astype(BF16)


def pieces_dot(dense, pieces, starts, first, rows, name):
    block = 256
    side = dense.shape[1]
    width = pieces[0].shape[1]
    return pl.pallas_call(
        lambda *refs: pieces_dot_kernel(starts, *refs),
        out_shape=jax.ShapeDtypeStruct((rows, width), BF16),
        grid=(rows // block,),
        in_specs=[pl.BlockSpec((block, side), lambda g: (g + first // block, 0))]
        + [pl.BlockSpec(p.shape, lambda g: (0, 0)) for p in pieces],
        out_specs=pl.BlockSpec((block, width), lambda g: (g, 0)),
        compiler_params=pltpu.CompilerParams(vmem_limit_bytes=28 * MIB),
        cost_estimate=pl.CostEstimate(
            flops=2 * rows * side * width, bytes_accessed=2 * rows * side, transcendentals=0
        ),
        name=name,
    )(dense, *pieces)


def layer_kernel(agg_ref, weight_ref, cot_ref, act_ref, pre_grad_ref, row_grad_ref):
    pre_act = jnp.dot(agg_ref[...], weight_ref[...], preferred_element_type=F32)
    gate = 1.0 / (1.0 + jnp.exp(-pre_act))
    act_ref[...] = (pre_act * gate).astype(BF16)
    slope = gate * (1.0 + pre_act * (1.0 - gate))
    pre_grad = (cot_ref[...].astype(F32) * slope).astype(BF16)
    pre_grad_ref[...] = pre_grad
    row_grad_ref[...] = lax.dot_general(
        pre_grad, weight_ref[...], (((1,), (1,)), ((), ())), preferred_element_type=F32
    ).astype(BF16)


def layer(aggregated, weight, cotangent):
    shape = jax.ShapeDtypeStruct(aggregated.shape, BF16)
    return pl.pallas_call(
        layer_kernel, out_shape=(shape, shape, shape), name="layer"
    )(aggregated, weight, cotangent)


def swap_core(value):
    return lax.ppermute(value, "row", [(r, r ^ 1) for r in range(16)])


def swap_half(value):
    return lax.ppermute(value, "row", [(r, r ^ 8) for r in range(16)])


def along_x(value, ahead):
    perm = []
    for r in range(16):
        half, x, core = r >> 3, (r >> 1) & 3, r & 1
        step = 1 if (core == 0) == ahead else -1
        perm.append((r, half * 8 + ((x + step) % 4) * 2 + core))
    return lax.ppermute(value, "row", perm)


def along_z(value, step):
    return lax.ppermute(value, "col", [(z, (z + step) % 8) for z in range(8)])


def swap_rep(value):
    return lax.ppermute(value, "rep", [(0, 1), (1, 0)])


def column_places(tile_columns):
    me = lax.axis_index("row")
    half, x, core = me >> 3, (me >> 1) & 3, me & 1
    dy = (tile_columns >> 3) ^ half
    dc = (tile_columns & 1) ^ core
    dx = (((tile_columns >> 1) & 3) - x) & 3
    e = jnp.where(core == 0, dx, (-dx) & 3)
    base = jnp.where(
        e == 0,
        2 * dc,
        jnp.where(e == 3, 4 + 2 * dc, jnp.where(e == 1, 10 + 2 * (1 - dc), 8 + 6 * dc)),
    )
    return base + dy


def row_places(tile_rows):
    z, low = lax.axis_index("col"), lax.axis_index("rep")
    dz = ((tile_rows >> 1) - z) & 7
    return 2 * dz + ((tile_rows & 1) ^ low)


def gather_row(own):
    pair = jnp.concatenate([own, swap_half(own)], 0)
    other = swap_core(pair)
    chip = jnp.concatenate([pair, other], 0)
    side = along_x(chip, True)
    far = along_x(side[:256], True)
    side_other = swap_core(side)
    far_other = swap_core(far)
    return (chip, side, far, side_other, far_other), (0, 512, 1024, 1280, 1792)


def scatter_row(part):
    far_other = swap_core(part[1792:2048])
    side_other = swap_core(part[1280:1792])
    far = along_x(wide_sum(part[1024:1280], far_other), False)
    side = jnp.concatenate(
        [wide_sum(part[512:768], side_other[:256], far), wide_sum(part[768:1024], side_other[256:])], 0
    )
    chip = along_x(side, False)
    mine = part[:256].astype(F32) + chip[:256].astype(F32)
    theirs = swap_core(wide_sum(part[256:512], chip[256:]))
    kept = swap_half(wide_sum(mine[128:], theirs[128:]))
    return wide_sum(mine[:128], theirs[:128], kept)


def scatter_col(block_of):
    middle = block_of(4)
    up = along_z(middle[:128], 1)
    down = along_z(middle[128:], -1)
    for d in (3, 2, 1):
        ahead, behind = block_of(d), block_of(8 - d)
        if d == 3:
            up_sum = jnp.concatenate([wide_sum(ahead[:128], up), ahead[128:]], 0)
            down_sum = jnp.concatenate([behind[:128], wide_sum(behind[128:], down)], 0)
        else:
            up_sum, down_sum = wide_sum(ahead, up), wide_sum(behind, down)
        up, down = along_z(up_sum, 1), along_z(down_sum, -1)
    here = block_of(0)
    theirs = swap_rep(wide_sum(here[128:], up[128:], down[128:]))
    return wide_sum(here[:128], up[:128], down[:128], theirs)


def gather_col(own):
    here = jnp.concatenate([own, swap_rep(own)], 0)
    from_up, from_down = [here], [here]
    for step in range(3):
        from_down.append(along_z(from_down[-1], 1))
        from_up.append(along_z(from_up[-1], -1))
    far_down = along_z(from_down[3][:128], 1)
    far_up = along_z(from_up[3][128:], -1)
    pieces = (here, from_up[1], from_up[2], from_up[3], far_down, far_up)
    pieces += (from_down[3], from_down[2], from_down[1])
    return pieces, (0, 256, 512, 768, 1024, 1152, 1280, 1536, 1792)


def keep_half(total, bit, swap):
    rows = total.shape[0] // 2
    kept = lax.dynamic_slice_in_dim(total, bit * rows, rows, 0)
    sent = lax.dynamic_slice_in_dim(total, (1 - bit) * rows, rows, 0).astype(BF16)
    return kept + swap(sent).astype(F32)


def swap_row(value, mask):
    return lax.ppermute(value, "row", [(r, r ^ mask) for r in range(16)])


def swap_z(value, mask):
    return lax.ppermute(value, "col", [(z, z ^ mask) for z in range(8)])


def join_halves(mine, bit, swap):
    theirs = swap(mine)
    low = jnp.where(bit == 0, mine, theirs)
    high = jnp.where(bit == 0, theirs, mine)
    return jnp.concatenate([low, high], 0)


ROW_MASKS = (1, 2, 4, 8)


def weight_share(local):
    me = lax.axis_index("row")
    for mask in ROW_MASKS:
        bit = (me // mask) & 1
        local = keep_half(local, bit, lambda v, mask=mask: swap_row(v, mask))
    share = local.astype(BF16)
    share = wide_sum(share, swap_rep(share))
    for mask in (1, 2, 4):
        share = wide_sum(share, swap_z(share, mask))
    return share


def weight_whole(share):
    me = lax.axis_index("row")
    for mask in ROW_MASKS[::-1]:
        bit = (me // mask) & 1
        share = join_halves(share, bit, lambda v, mask=mask: swap_row(v, mask))
    return share.astype(F32)


def body(features, tile_values, tile_coords, tile_counts, weight, cotangent):
    nodes = features.shape[0] * 256
    places = jnp.stack([row_places(tile_coords[:, 0]), column_places(tile_coords[:, 1])], -1)
    side = 2048
    dense = dense_block(tile_values, places, tile_counts, side, False)
    flipped = dense_block(tile_values, places, tile_counts, side, True)
    panel, starts = gather_row(features)
    first = pieces_dot(dense, panel, starts, 1024, 256, "rows_far")
    rest_high = pieces_dot(dense, panel, starts, 1280, 768, "rows_behind")
    rest_low = pieces_dot(dense, panel, starts, 0, 1024, "rows_ahead")

    def block_of(d):
        if d == 4:
            return first
        if d > 4:
            return rest_high[256 * (d - 5) : 256 * (d - 4)]
        return rest_low[256 * d : 256 * (d + 1)]

    aggregated = scatter_col(block_of)
    activations, pre_grad, own_grad = layer(aggregated, weight, cotangent)
    row_grad, depths = gather_col(own_grad)
    weight_local = lax.dot_general(
        aggregated, pre_grad, (((0,), (0,)), ((), ())), preferred_element_type=F32
    )
    grad_weight = weight_whole(weight_share(weight_local)) * lax.rsqrt(F32(nodes))
    column_part = pieces_dot(flipped, row_grad, depths, 0, side, "columns")
    grad_features = scatter_row(column_part)
    return (activations, grad_features, grad_weight)


def solution(mesh):
    split = ("row", "col", "rep")
    placed = (P(split, None), P(split, None, None), P(split, None), P(split), P(), P(split, None))
    return jax.shard_map(
        body,
        mesh=mesh,
        in_specs=placed,
        out_specs=(P(split, None), P(split, None), P()),
        check_vma=False,
    )
```

time: 686 us -> 199 us (0.29)
  waiting for transfers between devices: 422 us -> 73.7 us
  other arithmetic: 157 us -> 6.35 us
  starting transfers between devices: 0.2 us -> 70.7 us
  matrix products: 62.1 us -> 1.32 us
  Pallas kernels: 0 us -> 28.5 us
  local copies, waits for them, and re-layouts: 28.1 us -> 14.4 us
  between operations: 14.5 us -> 1.84 us
    scatter-add x8 -> x0, other arithmetic: 147 us -> none  [one_bunch(): return running.at[target].add(products * live_block[:, None, None])]
    psum x1 -> x0, waiting for transfers between devices: 147 us -> none  [sum_weights(): return lax.psum(weight_local, ('row', 'col', 'rep'))]
    reduce_scatter x2 -> x0, waiting for transfers between devices: 143 us -> none  [the longest x1 79.8 us: body(): lax.psum_scatter(column_part, 'row', scatter_dimension=0, tiled=True)]
    all_gather x2 -> x0, waiting for transfers between devices: 132 us -> none  [the longest x1 71.7 us: body(): row_grad = lax.all_gather(own_grad, ('col', 'rep'), axis=0, tiled=True)]
    ppermute x0 -> x42, waiting for transfers between devices: none -> 73.7 us  [the longest x16 26.4 us: along_z(): return lax.ppermute(value, 'col', [(z, (z + step) % 8) for z in range(8)])]
    ppermute x0 -> x42, starting transfers between devices: none -> 70.7 us  [the longest x16 25.5 us: along_z(): return lax.ppermute(value, 'col', [(z, (z + step) % 8) for z in range(8)])]
    dot_general x11 -> x1, matrix products: 62.1 us -> 1.32 us  [body(): lax.dot_general(aggregated, pre_grad, (((0,), (0,)), ((), ())), preferred...]
    pallas_call x0 -> x7, Pallas kernels: none -> 28.5 us  [the longest x2 14.4 us: dense_block(): pl.pallas_call(lambda *refs: dense_kernel(flip, *refs), out_shape=jax.Sha...]
  transfers between devices with their start and end apart: 5 -> 42, of which waited for: 5 -> 26; matrix products, arithmetic and copies ran while one was open for 18% -> 2% of each run, Pallas kernels for 0% -> 13%
where the time goes in v1:
time: 199 us; the launch traced here: 197 us
  waiting for transfers between devices  73.7 us (37%)
  starting transfers between devices  70.7 us (36%)
  Pallas kernels  28.5 us (14%)
  local copies, waits for them, and re-layouts  14.4 us (7%)
  other arithmetic  6.35 us (3%)
    ppermute x16, waiting for transfers between devices, along_z(): return lax.ppermute(value, 'col', [(z, (z + step) % 8) for z in range(8)])  26.4 us
    ppermute x16, starting transfers between devices, along_z(): return lax.ppermute(value, 'col', [(z, (z + step) % 8) for z in range(8)])  25.5 us
    ppermute x8, waiting for transfers between devices, swap_row(): return lax.ppermute(value, 'row', [(r, r ^ mask) for r in range(16)])  21.7 us
    ppermute x8, starting transfers between devices, swap_row(): return lax.ppermute(value, 'row', [(r, r ^ mask) for r in range(16)])  17.3 us
    ppermute x4, waiting for transfers between devices, along_x(): return lax.ppermute(value, 'row', perm)  14.7 us
    pallas_call x2, Pallas kernels, dense_block(): pl.pallas_call(lambda *refs: dense_kernel(flip, *refs), out_shape=jax.Sha...  14.4 us
    ppermute x6, starting transfers between devices, swap_core(): return lax.ppermute(value, 'row', [(r, r ^ 1) for r in range(16)])  14.2 us
    unnamed x23, local copies, waits for them, and re-layouts  13.9 us
  transfers between devices with their start and end apart: 42, of which 26 were waited for; matrix products, arithmetic and copies ran while one was open for 2% of the time, Pallas kernels for 13%

profile of v1, /device:TPU:1, one launch (start us, length us, event | category | flops | bytes accessed | tf_op | source)
XLA Modules:
  0.0 196.9 jit_solution(9908996230297974919)
XLA Ops:
  0.6 3.8 %collective-permute-start = (bf16[128,512]{1,0:T(8,128)(2,1)}, bf16[128,512]{1,0:T(8,128)(2,1)S(1)}, u32[]{:S(2)}, u32[]{:S(2)}) collective-permute-start(bf16[128,512]{1,0:T(8,128)(2,1)} %param.6), channel_id=1, source_target_pairs={{0,128},{16,144},{32,160},{48,176},{64,192},{80,208},{96,224},{112... | collective-permute-start | bytes 393224 | tf_op jit(solution)/shard_map/ppermute | solution.py:119
  4.5 2.6 %collective-permute-done = bf16[128,512]{1,0:T(8,128)(2,1)S(1)} collective-permute-done((bf16[128,512]{1,0:T(8,128)(2,1)}, bf16[128,512]{1,0:T(8,128)(2,1)S(1)}, u32[]{:S(2)}, u32[]{:S(2)}) %collective-permute-start) | collective-permute-done | bytes 131104 | tf_op jit(solution)/shard_map/ppermute | solution.py:119
  7.0 0.9 pad_maximum_fusion.1
  8.0 3.7 %collective-permute-start.1 = (bf16[256,512]{1,0:T(8,128)(2,1)S(1)}, bf16[256,512]{1,0:T(8,128)(2,1)S(1)}, u32[]{:S(2)}, u32[]{:S(2)}) collective-permute-start(bf16[256,512]{1,0:T(8,128)(2,1)S(1)} %pad_maximum_fusion.1), channel_id=1, source_target_pairs={{0,16},{16,0},{32,48},{48,32},{64,80},{80,64},{96,112},{112,96},{1... | collective-permute-start | bytes 786440 | tf_op jit(solution)/shard_map/ppermute | solution.py:115
  11.7 0.9 constant_dynamic-update-slice_fusion.2
  12.8 1.1 collective-permute-start.2
  13.9 7.3 %collective-permute-done.2.refs_2_ = bf16[512,512]{1,0:T(8,128)(2,1)S(1)} collective-permute-done((bf16[512,512]{1,0:T(8,128)(2,1)S(1)}, bf16[512,512]{1,0:T(8,128)(2,1)S(1)}, u32[]{:S(2)}, u32[]{:S(2)}) %collective-permute-start.2) | collective-permute-done | bytes 524320 | tf_op jit(solution)/shard_map/ppermute | solution.py:128
  21.3 2.0 %collective-permute-start.3 = (bf16[256,512]{1,0:T(8,128)(2,1)S(1)}, bf16[256,512]{1,0:T(8,128)(2,1)S(1)}, u32[]{:S(2)}, u32[]{:S(2)}) collective-permute-start(bf16[256,512]{1,0:T(8,128)(2,1)S(1)} %slice.153), channel_id=1, source_target_pairs={{0,32},{16,112},{32,64},{48,16},{64,96},{80,48},{96,0},{112,80},{1... | collective-permute-start | bytes 786440 | tf_op jit(solution)/shard_map/ppermute | solution.py:128
  24.5 2.0 %collective-permute-done.3.refs_3_ = bf16[256,512]{1,0:T(8,128)(2,1)S(1)} collective-permute-done((bf16[256,512]{1,0:T(8,128)(2,1)S(1)}, bf16[256,512]{1,0:T(8,128)(2,1)S(1)}, u32[]{:S(2)}, u32[]{:S(2)}) %collective-permute-start.3) | collective-permute-done | bytes 262176 | tf_op jit(solution)/shard_map/ppermute | solution.py:128
  26.6 4.8 %collective-permute-start.5 = (bf16[256,512]{1,0:T(8,128)(2,1)S(1)}, bf16[256,512]{1,0:T(8,128)(2,1)S(1)}, u32[]{:S(2)}, u32[]{:S(2)}) collective-permute-start(bf16[256,512]{1,0:T(8,128)(2,1)S(1)} %collective-permute-done.3.refs_3_), channel_id=1, source_target_pairs={{0,16},{16,0},{32,48},{48,32},{64,80},{80,64},{96,112},{112,96},{1... | collective-permute-start | bytes 786440 | tf_op jit(solution)/shard_map/ppermute | solution.py:115
  31.7 2.2 %copy-done = bf16[128,128,128]{2,1,0:T(8,128)(2,1)S(1)} copy-done((bf16[128,128,128]{2,1,0:T(8,128)(2,1)S(1)}, bf16[128,128,128]{2,1,0:T(8,128)(2,1)}, u32[]{:S(2)}) %copy-start) | copy-done | bytes 4194328
  33.9 3.9 %dense_build.1.refs_0_ = bf16[2048,2048]{1,0:T(8,128)(2,1)S(1)} custom-call(s32[1]{0:T(128)S(6)} %copy.13.refs_0_, s32[256]{0:T(256)S(1)} %reshape.10.refs_1_, bf16[128,128,128]{2,1,0:T(8,128)(2,1)S(1)} %copy-done), custom_call_target="tpu_custom_call" | custom-call | bytes 12582912 | tf_op jit(solution)/shard_map/dense_build/pallas_call | solution.py:49
  38.5 3.9 %collective-permute-start.10 = (bf16[128,512]{1,0:T(8,128)(2,1)S(1)}, bf16[128,512]{1,0:T(8,128)(2,1)S(1)}, u32[]{:S(2)}, u32[]{:S(2)}) collective-permute-start(bf16[128,512]{1,0:T(8,128)(2,1)S(1)} %get-tuple-element.18), channel_id=1, source_target_pairs={{0,14},{2,0},{4,2},{6,4},{8,6},{10,8},{12,10},{14,12},{1,15},{3,1}... | collective-permute-start | bytes 393224 | tf_op jit(solution)/shard_map/ppermute | solution.py:132
  42.4 2.1 %rows_behind.1 = bf16[768,512]{1,0:T(8,128)(2,1)S(1)} custom-call(bf16[2048,2048]{1,0:T(8,128)(2,1)S(1)} %dense_build.1.refs_0_, bf16[512,512]{1,0:T(8,128)(2,1)S(1)} %constant_dynamic-update-slice_fusion.refs_1_, bf16[512,512]{1,0:T(8,128)(2,1)S(1)} %collective-permute-done.2.refs_2_, bf16[256,512]{1,0:T(8,128)(2,1)S(1)} %collective-permute-done.3.refs_3_, ...), custom_call_target="tpu_custom_call" | custom-call | flops 1610612736 | bytes 3145728 | tf_op jit(solution)/shard_map/rows_behind/pallas_call | solution.py:80
  44.5 2.9 %rows_ahead.1 = bf16[1024,512]{1,0:T(8,128)(2,1)S(1)} custom-call(bf16[2048,2048]{1,0:T(8,128)(2,1)S(1)} %dense_build.1.refs_0_, bf16[512,512]{1,0:T(8,128)(2,1)S(1)} %constant_dynamic-update-slice_fusion.refs_1_, bf16[512,512]{1,0:T(8,128)(2,1)S(1)} %collective-permute-done.2.refs_2_, bf16[256,512]{1,0:T(8,128)(2,1)S(1)} %collective-permute-done.3.refs_3_, ...), custom_call_target="tpu_custom_call" | custom-call | flops 2147483648 | bytes 4194304 | tf_op jit(solution)/shard_map/rows_ahead/pallas_call | solution.py:80
  47.6 2.7 %collective-permute-start.11 = (bf16[256,512]{1,0:T(8,128)(2,1)S(1)}, bf16[256,512]{1,0:T(8,128)(2,1)S(1)}, u32[]{:S(2)}, u32[]{:S(2)}) collective-permute-start(bf16[256,512]{1,0:T(8,128)(2,1)S(1)} %pad_maximum_fusion.3), channel_id=1, source_target_pairs={{0,14},{2,0},{4,2},{6,4},{8,6},{10,8},{12,10},{14,12},{1,15},{3,1}... | collective-permute-start | bytes 786440 | tf_op jit(solution)/shard_map/ppermute | solution.py:132
  50.3 3.0 %collective-permute-done.6 = bf16[128,512]{1,0:T(8,128)(2,1)S(1)} collective-permute-done((bf16[128,512]{1,0:T(8,128)(2,1)S(1)}, bf16[128,512]{1,0:T(8,128)(2,1)S(1)}, u32[]{:S(2)}, u32[]{:S(2)}) %collective-permute-start.6) | collective-permute-done | bytes 131104 | tf_op jit(solution)/shard_map/ppermute | solution.py:132
  53.5 1.7 collective-permute-done.11
  55.3 3.5 %collective-permute-start.12 = (bf16[256,512]{1,0:T(8,128)(2,1)S(1)}, bf16[256,512]{1,0:T(8,128)(2,1)S(1)}, u32[]{:S(2)}, u32[]{:S(2)}) collective-permute-start(bf16[256,512]{1,0:T(8,128)(2,1)S(1)} %add_convert_fusion.5), channel_id=1, source_target_pairs={{0,14},{2,0},{4,2},{6,4},{8,6},{10,8},{12,10},{14,12},{1,15},{3,1}... | collective-permute-start | bytes 786440 | tf_op jit(solution)/shard_map/ppermute | solution.py:132
  58.8 2.4 %collective-permute-done.7 = bf16[256,512]{1,0:T(8,128)(2,1)S(1)} collective-permute-done((bf16[256,512]{1,0:T(8,128)(2,1)S(1)}, bf16[256,512]{1,0:T(8,128)(2,1)S(1)}, u32[]{:S(2)}, u32[]{:S(2)}) %collective-permute-start.7) | collective-permute-done | bytes 262176 | tf_op jit(solution)/shard_map/ppermute | solution.py:132
  61.4 1.4 collective-permute-done.12
  62.9 3.5 %collective-permute-start.13 = (bf16[256,512]{1,0:T(8,128)(2,1)S(1)}, bf16[256,512]{1,0:T(8,128)(2,1)S(1)}, u32[]{:S(2)}, u32[]{:S(2)}) collective-permute-start(bf16[256,512]{1,0:T(8,128)(2,1)S(1)} %add_convert_fusion.4), channel_id=1, source_target_pairs={{0,14},{2,0},{4,2},{6,4},{8,6},{10,8},{12,10},{14,12},{1,15},{3,1}... | collective-permute-start | bytes 786440 | tf_op jit(solution)/shard_map/ppermute | solution.py:132
  66.3 1.8 collective-permute-done.8
  68.5 1.2 collective-permute-done.13
  69.7 5.3 %collective-permute-done.9 = bf16[256,512]{1,0:T(8,128)(2,1)S(1)} collective-permute-done((bf16[256,512]{1,0:T(8,128)(2,1)S(1)}, bf16[256,512]{1,0:T(8,128)(2,1)S(1)}, u32[]{:S(2)}, u32[]{:S(2)}) %collective-permute-start.9) | collective-permute-done | bytes 262176 | tf_op jit(solution)/shard_map/ppermute | solution.py:132
  75.0 2.6 %collective-permute-start.14 = (bf16[128,512]{1,0:T(8,128)(2,1)S(1)}, bf16[128,512]{1,0:T(8,128)(2,1)S(1)}, u32[]{:S(2)}, u32[]{:S(2)}) collective-permute-start(bf16[128,512]{1,0:T(8,128)(2,1)S(1)} %add_convert_fusion.9), channel_id=1, source_target_pairs={{0,1},{1,0},{2,3},{3,2},{4,5},{5,4},{6,7},{7,6},{8,9},{9,8},{10,11... | collective-permute-start | bytes 393224 | tf_op jit(solution)/shard_map/ppermute | solution.py:136
  77.5 2.4 %collective-permute-done.14 = bf16[128,512]{1,0:T(8,128)(2,1)S(1)} collective-permute-done((bf16[128,512]{1,0:T(8,128)(2,1)S(1)}, bf16[128,512]{1,0:T(8,128)(2,1)S(1)}, u32[]{:S(2)}, u32[]{:S(2)}) %collective-permute-start.14) | collective-permute-done | bytes 131104 | tf_op jit(solution)/shard_map/ppermute | solution.py:136
  79.9 0.7 add_convert_fusion.8.agg_ref
  80.6 2.2 %layer.1 = (bf16[128,512]{1,0:T(8,128)(2,1)}, bf16[128,512]{1,0:T(8,128)(2,1)}, bf16[128,512]{1,0:T(8,128)(2,1)}) custom-call(bf16[128,512]{1,0:T(8,128)(2,1)} %add_convert_fusion.8.agg_ref, bf16[512,512]{1,0:T(8,128)(2,1)} %weight_ref.1, bf16[128,512]{1,0:T(8,128)(2,1)} %cot_ref.1), custom_call_target="tpu_custom_call" | custom-call | tf_op jit(solution)/shard_map/layer/pallas_call | solution.py:109
  82.9 1.3 fusion.5
  84.2 4.9 %collective-permute-start.30 = (bf16[256,512]{1,0:T(8,128)(2,1)S(1)}, bf16[256,512]{1,0:T(8,128)(2,1)S(1)}, u32[]{:S(2)}, u32[]{:S(2)}) collective-permute-start(bf16[256,512]{1,0:T(8,128)(2,1)S(1)} %dynamic-slice_convert_fusion), channel_id=1, source_target_pairs={{0,16},{16,0},{32,48},{48,32},{64,80},{80,64},{96,112},{112,96},{1... | collective-permute-start | bytes 786440 | tf_op jit(solution)/shard_map/ppermute | solution.py:223
  89.1 1.2 collective-permute-done.30
  90.5 4.7 %collective-permute-done.31 = bf16[128,512]{1,0:T(8,128)(2,1)S(1)} collective-permute-done((bf16[128,512]{1,0:T(8,128)(2,1)S(1)}, bf16[128,512]{1,0:T(8,128)(2,1)S(1)}, u32[]{:S(2)}, u32[]{:S(2)}) %collective-permute-start.31) | collective-permute-done | bytes 131104 | tf_op jit(solution)/shard_map/ppermute | solution.py:223
  95.9 4.0 %collective-permute-done.32 = bf16[64,512]{1,0:T(8,128)(2,1)S(1)} collective-permute-done((bf16[64,512]{1,0:T(8,128)(2,1)S(1)}, bf16[64,512]{1,0:T(8,128)(2,1)S(1)}, u32[]{:S(2)}, u32[]{:S(2)}) %collective-permute-start.32) | collective-permute-done | bytes 65568 | tf_op jit(solution)/shard_map/ppermute | solution.py:223
  100.0 4.1 %collective-permute-start.33 = (bf16[32,512]{1,0:T(8,128)(2,1)S(1)}, bf16[32,512]{1,0:T(8,128)(2,1)S(1)}, u32[]{:S(2)}, u32[]{:S(2)}) collective-permute-start(bf16[32,512]{1,0:T(8,128)(2,1)S(1)} %dynamic-slice_convert_fusion.3), channel_id=1, source_target_pairs={{0,128},{16,144},{32,160},{48,176},{64,192},{80,208},{96,224},{112... | collective-permute-start | bytes 98312 | tf_op jit(solution)/shard_map/ppermute | solution.py:223
  104.3 1.2 collective-permute-done.33
  105.5 0.7 collective-permute-start.34
  106.2 2.3 %collective-permute-done.15 = bf16[128,512]{1,0:T(8,128)(2,1)S(1)} collective-permute-done((bf16[128,512]{1,0:T(8,128)(2,1)S(1)}, bf16[128,512]{1,0:T(8,128)(2,1)S(1)}, u32[]{:S(2)}, u32[]{:S(2)}) %collective-permute-start.15) | collective-permute-done | bytes 131104 | tf_op jit(solution)/shard_map/ppermute | solution.py:136
  108.6 2.7 %collective-permute-start.16 = (bf16[256,512]{1,0:T(8,128)(2,1)S(1)}, bf16[256,512]{1,0:T(8,128)(2,1)S(1)}, u32[]{:S(2)}, u32[]{:S(2)}) collective-permute-start(bf16[256,512]{1,0:T(8,128)(2,1)S(1)} %constant_dynamic-update-slice_fusion.3.refs_1_), channel_id=1, source_target_pairs={{0,14},{2,0},{4,2},{6,4},{8,6},{10,8},{12,10},{14,12},{1,15},{3,1}... | collective-permute-start | bytes 786440 | tf_op jit(solution)/shard_map/ppermute | solution.py:132
  111.4 3.6 %collective-permute-done.19.refs_9_ = bf16[256,512]{1,0:T(8,128)(2,1)S(1)} collective-permute-done((bf16[256,512]{1,0:T(8,128)(2,1)S(1)}, bf16[256,512]{1,0:T(8,128)(2,1)S(1)}, u32[]{:S(2)}, u32[]{:S(2)}) %collective-permute-start.19) | collective-permute-done | bytes 262176 | tf_op jit(solution)/shard_map/ppermute | solution.py:132
  115.0 2.7 %collective-permute-start.17 = (bf16[256,512]{1,0:T(8,128)(2,1)S(1)}, bf16[256,512]{1,0:T(8,128)(2,1)S(1)}, u32[]{:S(2)}, u32[]{:S(2)}) collective-permute-start(bf16[256,512]{1,0:T(8,128)(2,1)S(1)} %collective-permute-done.16.refs_2_), channel_id=1, source_target_pairs={{0,14},{2,0},{4,2},{6,4},{8,6},{10,8},{12,10},{14,12},{1,15},{3,1}... | collective-permute-start | bytes 786440 | tf_op jit(solution)/shard_map/ppermute | solution.py:132
  117.8 3.8 %collective-permute-done.20.refs_8_ = bf16[256,512]{1,0:T(8,128)(2,1)S(1)} collective-permute-done((bf16[256,512]{1,0:T(8,128)(2,1)S(1)}, bf16[256,512]{1,0:T(8,128)(2,1)S(1)}, u32[]{:S(2)}, u32[]{:S(2)}) %collective-permute-start.20) | collective-permute-done | bytes 262176 | tf_op jit(solution)/shard_map/ppermute | solution.py:132
  121.7 2.9 %collective-permute-start.18 = (bf16[256,512]{1,0:T(8,128)(2,1)S(1)}, bf16[256,512]{1,0:T(8,128)(2,1)S(1)}, u32[]{:S(2)}, u32[]{:S(2)}) collective-permute-start(bf16[256,512]{1,0:T(8,128)(2,1)S(1)} %collective-permute-done.17.refs_3_), channel_id=1, source_target_pairs={{0,14},{2,0},{4,2},{6,4},{8,6},{10,8},{12,10},{14,12},{1,15},{3,1}... | collective-permute-start | bytes 786440 | tf_op jit(solution)/shard_map/ppermute | solution.py:132
  125.2 2.2 %copy-done.1 = bf16[128,128,128]{2,1,0:T(8,128)(2,1)S(1)} copy-done((bf16[128,128,128]{2,1,0:T(8,128)(2,1)S(1)}, bf16[128,128,128]{2,1,0:T(8,128)(2,1)}, u32[]{:S(2)}) %copy-start.1) | copy-done | bytes 4194328
  127.4 10.5 %flipped_build.1.refs_0_ = bf16[2048,2048]{1,0:T(8,128)(2,1)S(1)} custom-call(s32[1]{0:T(128)S(6)} %copy.13.refs_0_, s32[256]{0:T(256)S(1)} %reshape.10.refs_1_, bf16[128,128,128]{2,1,0:T(8,128)(2,1)S(1)} %copy-done.1), custom_call_target="tpu_custom_call" | custom-call | bytes 12582912 | tf_op jit(solution)/shard_map/flipped_build/pallas_call | solution.py:49
  138.0 3.3 %copy-done.2 = bf16[2048,2048]{1,0:T(8,128)(2,1)} copy-done((bf16[2048,2048]{1,0:T(8,128)(2,1)}, bf16[2048,2048]{1,0:T(8,128)(2,1)S(1)}, u32[]{:S(2)}) %copy-start.2) | copy-done | bytes 8388632
  141.6 2.7 %collective-permute-start.23 = (bf16[128,512]{1,0:T(8,128)(2,1)S(1)}, bf16[128,512]{1,0:T(8,128)(2,1)S(1)}, u32[]{:S(2)}, u32[]{:S(2)}) collective-permute-start(bf16[128,512]{1,0:T(8,128)(2,1)S(1)} %slice.171), channel_id=1, source_target_pairs={{0,14},{2,0},{4,2},{6,4},{8,6},{10,8},{12,10},{14,12},{1,15},{3,1}... | collective-permute-start | bytes 393224 | tf_op jit(solution)/shard_map/ppermute | solution.py:132
  144.5 2.1 %collective-permute-done.22.refs_5_ = bf16[128,512]{1,0:T(8,128)(2,1)S(1)} collective-permute-done((bf16[128,512]{1,0:T(8,128)(2,1)S(1)}, bf16[128,512]{1,0:T(8,128)(2,1)S(1)}, u32[]{:S(2)}, u32[]{:S(2)}) %collective-permute-start.22) | collective-permute-done | bytes 131104 | tf_op jit(solution)/shard_map/ppermute | solution.py:132
  146.6 3.4 %copy-done.3 = bf16[2048,2048]{1,0:T(8,128)(2,1)S(1)} copy-done((bf16[2048,2048]{1,0:T(8,128)(2,1)S(1)}, bf16[2048,2048]{1,0:T(8,128)(2,1)}, u32[]{:S(2)}) %copy-start.3) | copy-done | bytes 8388632
  150.0 0.9 copy-done.5
  150.9 0.9 copy-done.7
  151.9 6.2 %columns.1 = bf16[2048,512]{1,0:T(8,128)(2,1)S(1)} custom-call(bf16[2048,2048]{1,0:T(8,128)(2,1)S(1)} %copy-done.3, bf16[256,512]{1,0:T(8,128)(2,1)S(1)} %constant_dynamic-update-slice_fusion.3.refs_1_, bf16[256,512]{1,0:T(8,128)(2,1)S(1)} %collective-permute-done.16.refs_2_, bf16[256,512]{1,0:T(8,128)(2,1)S(1)} %copy-done.7, ...), custom_call_target="tpu_custom_call" | custom-call | flops 4294967296 | bytes 8388608 | tf_op jit(solution)/shard_map/columns/pallas_call | solution.py:80
  158.1 4.9 %collective-permute-start.25 = (bf16[256,512]{1,0:T(8,128)(2,1)S(1)}, bf16[256,512]{1,0:T(8,128)(2,1)S(1)}, u32[]{:S(2)}, u32[]{:S(2)}) collective-permute-start(bf16[256,512]{1,0:T(8,128)(2,1)S(1)} %slice.177), channel_id=1, source_target_pairs={{0,16},{16,0},{32,48},{48,32},{64,80},{80,64},{96,112},{112,96},{1... | collective-permute-start | bytes 786440 | tf_op jit(solution)/shard_map/ppermute | solution.py:115
  163.2 4.1 %collective-permute-start.39 = (bf16[64,512]{1,0:T(8,128)(2,1)S(1)}, bf16[64,512]{1,0:T(8,128)(2,1)S(1)}, u32[]{:S(2)}, u32[]{:S(2)}) collective-permute-start(bf16[64,512]{1,0:T(8,128)(2,1)S(1)} %pad_maximum_fusion.6), channel_id=1, source_target_pairs={{0,64},{16,80},{32,96},{48,112},{64,0},{80,16},{96,32},{112,48},{1... | collective-permute-start | bytes 196616 | tf_op jit(solution)/shard_map/ppermute | solution.py:223
  167.3 0.8 add_convert_fusion.3
  168.0 1.4 collective-permute-done.39
  169.4 5.4 %collective-permute-done.26 = bf16[256,512]{1,0:T(8,128)(2,1)} collective-permute-done((bf16[256,512]{1,0:T(8,128)(2,1)}, bf16[256,512]{1,0:T(8,128)(2,1)}, u32[]{:S(2)}, u32[]{:S(2)}) %collective-permute-start.26) | collective-permute-done | bytes 262176 | tf_op jit(solution)/shard_map/ppermute | solution.py:128
  174.8 1.1 add_convert_fusion.2
  176.6 8.3 %collective-permute-done.40 = bf16[128,512]{1,0:T(8,128)(2,1)S(1)} collective-permute-done((bf16[128,512]{1,0:T(8,128)(2,1)S(1)}, bf16[128,512]{1,0:T(8,128)(2,1)S(1)}, u32[]{:S(2)}, u32[]{:S(2)}) %collective-permute-start.40) | collective-permute-done | bytes 131104 | tf_op jit(solution)/shard_map/ppermute | solution.py:223
  185.1 2.8 %collective-permute-start.41 = (bf16[256,512]{1,0:T(8,128)(2,1)S(1)}, bf16[256,512]{1,0:T(8,128)(2,1)S(1)}, u32[]{:S(2)}, u32[]{:S(2)}) collective-permute-start(bf16[256,512]{1,0:T(8,128)(2,1)S(1)} %pad_maximum_fusion.4), channel_id=1, source_target_pairs={{0,16},{16,0},{32,48},{48,32},{64,80},{80,64},{96,112},{112,96},{1... | collective-permute-start | bytes 786440 | tf_op jit(solution)/shard_map/ppermute | solution.py:223
  188.1 0.9 collective-permute-done.41
  189.6 2.5 %collective-permute-start.29 = (bf16[128,512]{1,0:T(8,128)(2,1)S(1)}, bf16[128,512]{1,0:T(8,128)(2,1)S(1)}, u32[]{:S(2)}, u32[]{:S(2)}) collective-permute-start(bf16[128,512]{1,0:T(8,128)(2,1)S(1)} %fusion), channel_id=1, source_target_pairs={{0,128},{16,144},{32,160},{48,176},{64,192},{80,208},{96,224},{112... | collective-permute-start | bytes 393224 | tf_op jit(solution)/shard_map/ppermute | solution.py:119
  192.2 1.1 convert_multiply_fusion
  193.3 2.9 %collective-permute-done.29 = bf16[128,512]{1,0:T(8,128)(2,1)S(1)} collective-permute-done((bf16[128,512]{1,0:T(8,128)(2,1)S(1)}, bf16[128,512]{1,0:T(8,128)(2,1)S(1)}, u32[]{:S(2)}, u32[]{:S(2)}) %collective-permute-start.29) | collective-permute-done | bytes 131104 | tf_op jit(solution)/shard_map/ppermute | solution.py:119
  (102 shorter events, 7.9 us)
Async XLA Ops:
  0.6 30.7 %copy-start.9 = (s32[128,2]{0,1:T(2,128)S(1)}, s32[128,2]{0,1:T(2,128)}, u32[]{:S(2)}) copy-start(s32[128,2]{0,1:T(2,128)} %param.8) | copy-start | bytes 3076
  0.6 6.4 %collective-permute-start = (bf16[128,512]{1,0:T(8,128)(2,1)}, bf16[128,512]{1,0:T(8,128)(2,1)S(1)}, u32[]{:S(2)}, u32[]{:S(2)}) collective-permute-start(bf16[128,512]{1,0:T(8,128)(2,1)} %param.6), channel_id=1, source_target_pairs={{0,128},{16,144},{32,160},{48,176},{64,192},{80,208},{96,224},{112... | collective-permute-start | bytes 393224 | tf_op jit(solution)/shard_map/ppermute | solution.py:119
  8.0 4.9 %collective-permute-start.1 = (bf16[256,512]{1,0:T(8,128)(2,1)S(1)}, bf16[256,512]{1,0:T(8,128)(2,1)S(1)}, u32[]{:S(2)}, u32[]{:S(2)}) collective-permute-start(bf16[256,512]{1,0:T(8,128)(2,1)S(1)} %pad_maximum_fusion.1), channel_id=1, source_target_pairs={{0,16},{16,0},{32,48},{48,32},{64,80},{80,64},{96,112},{112,96},{1... | collective-permute-start | bytes 786440 | tf_op jit(solution)/shard_map/ppermute | solution.py:115
  12.8 8.4 %collective-permute-start.2 = (bf16[512,512]{1,0:T(8,128)(2,1)S(1)}, bf16[512,512]{1,0:T(8,128)(2,1)S(1)}, u32[]{:S(2)}, u32[]{:S(2)}) collective-permute-start(bf16[512,512]{1,0:T(8,128)(2,1)S(1)} %constant_dynamic-update-slice_fusion.refs_1_), channel_id=1, source_target_pairs={{0,32},{16,112},{32,64},{48,16},{64,96},{80,48},{96,0},{112,80},{1... | collective-permute-start | bytes 1572872 | tf_op jit(solution)/shard_map/ppermute | solution.py:128
  21.3 5.3 %collective-permute-start.3 = (bf16[256,512]{1,0:T(8,128)(2,1)S(1)}, bf16[256,512]{1,0:T(8,128)(2,1)S(1)}, u32[]{:S(2)}, u32[]{:S(2)}) collective-permute-start(bf16[256,512]{1,0:T(8,128)(2,1)S(1)} %slice.153), channel_id=1, source_target_pairs={{0,32},{16,112},{32,64},{48,16},{64,96},{80,48},{96,0},{112,80},{1... | collective-permute-start | bytes 786440 | tf_op jit(solution)/shard_map/ppermute | solution.py:128
  23.3 14.5 %collective-permute-start.4 = (bf16[512,512]{1,0:T(8,128)(2,1)S(1)}, bf16[512,512]{1,0:T(8,128)(2,1)S(1)}, u32[]{:S(2)}, u32[]{:S(2)}) collective-permute-start(bf16[512,512]{1,0:T(8,128)(2,1)S(1)} %collective-permute-done.2.refs_2_), channel_id=1, source_target_pairs={{0,16},{16,0},{32,48},{48,32},{64,80},{80,64},{96,112},{112,96},{1... | collective-permute-start | bytes 1572872 | tf_op jit(solution)/shard_map/ppermute | solution.py:115
  26.6 11.2 %collective-permute-start.5 = (bf16[256,512]{1,0:T(8,128)(2,1)S(1)}, bf16[256,512]{1,0:T(8,128)(2,1)S(1)}, u32[]{:S(2)}, u32[]{:S(2)}) collective-permute-start(bf16[256,512]{1,0:T(8,128)(2,1)S(1)} %collective-permute-done.3.refs_3_), channel_id=1, source_target_pairs={{0,16},{16,0},{32,48},{48,32},{64,80},{80,64},{96,112},{112,96},{1... | collective-permute-start | bytes 786440 | tf_op jit(solution)/shard_map/ppermute | solution.py:115
  31.7 2.2 %copy-start = (bf16[128,128,128]{2,1,0:T(8,128)(2,1)S(1)}, bf16[128,128,128]{2,1,0:T(8,128)(2,1)}, u32[]{:S(2)}) copy-start(bf16[128,128,128]{2,1,0:T(8,128)(2,1)} %refs_2_.3) | copy-start | bytes 12582916
  38.5 9.0 %collective-permute-start.10 = (bf16[128,512]{1,0:T(8,128)(2,1)S(1)}, bf16[128,512]{1,0:T(8,128)(2,1)S(1)}, u32[]{:S(2)}, u32[]{:S(2)}) collective-permute-start(bf16[128,512]{1,0:T(8,128)(2,1)S(1)} %get-tuple-element.18), channel_id=1, source_target_pairs={{0,14},{2,0},{4,2},{6,4},{8,6},{10,8},{12,10},{14,12},{1,15},{3,1}... | collective-permute-start | bytes 393224 | tf_op jit(solution)/shard_map/ppermute | solution.py:132
  47.4 5.9 %collective-permute-start.6 = (bf16[128,512]{1,0:T(8,128)(2,1)S(1)}, bf16[128,512]{1,0:T(8,128)(2,1)S(1)}, u32[]{:S(2)}, u32[]{:S(2)}) collective-permute-start(bf16[128,512]{1,0:T(8,128)(2,1)S(1)} %get-tuple-element.17), channel_id=1, source_target_pairs={{0,2},{2,4},{4,6},{6,8},{8,10},{10,12},{12,14},{14,0},{1,3},{3,5},... | collective-permute-start | bytes 393224 | tf_op jit(solution)/shard_map/ppermute | solution.py:132
  47.6 7.7 %collective-permute-start.11 = (bf16[256,512]{1,0:T(8,128)(2,1)S(1)}, bf16[256,512]{1,0:T(8,128)(2,1)S(1)}, u32[]{:S(2)}, u32[]{:S(2)}) collective-permute-start(bf16[256,512]{1,0:T(8,128)(2,1)S(1)} %pad_maximum_fusion.3), channel_id=1, source_target_pairs={{0,14},{2,0},{4,2},{6,4},{8,6},{10,8},{12,10},{14,12},{1,15},{3,1}... | collective-permute-start | bytes 786440 | tf_op jit(solution)/shard_map/ppermute | solution.py:132
  53.4 7.8 %collective-permute-start.7 = (bf16[256,512]{1,0:T(8,128)(2,1)S(1)}, bf16[256,512]{1,0:T(8,128)(2,1)S(1)}, u32[]{:S(2)}, u32[]{:S(2)}) collective-permute-start(bf16[256,512]{1,0:T(8,128)(2,1)S(1)} %pad_maximum_fusion.2), channel_id=1, source_target_pairs={{0,2},{2,4},{4,6},{6,8},{8,10},{10,12},{12,14},{14,0},{1,3},{3,5},... | collective-permute-start | bytes 786440 | tf_op jit(solution)/shard_map/ppermute | solution.py:132
  55.3 7.5 %collective-permute-start.12 = (bf16[256,512]{1,0:T(8,128)(2,1)S(1)}, bf16[256,512]{1,0:T(8,128)(2,1)S(1)}, u32[]{:S(2)}, u32[]{:S(2)}) collective-permute-start(bf16[256,512]{1,0:T(8,128)(2,1)S(1)} %add_convert_fusion.5), channel_id=1, source_target_pairs={{0,14},{2,0},{4,2},{6,4},{8,6},{10,8},{12,10},{14,12},{1,15},{3,1}... | collective-permute-start | bytes 786440 | tf_op jit(solution)/shard_map/ppermute | solution.py:132
  61.3 6.9 %collective-permute-start.8 = (bf16[256,512]{1,0:T(8,128)(2,1)S(1)}, bf16[256,512]{1,0:T(8,128)(2,1)S(1)}, u32[]{:S(2)}, u32[]{:S(2)}) collective-permute-start(bf16[256,512]{1,0:T(8,128)(2,1)S(1)} %add_convert_fusion.7), channel_id=1, source_target_pairs={{0,2},{2,4},{4,6},{6,8},{8,10},{10,12},{12,14},{14,0},{1,3},{3,5},... | collective-permute-start | bytes 786440 | tf_op jit(solution)/shard_map/ppermute | solution.py:132
  62.9 6.8 %collective-permute-start.13 = (bf16[256,512]{1,0:T(8,128)(2,1)S(1)}, bf16[256,512]{1,0:T(8,128)(2,1)S(1)}, u32[]{:S(2)}, u32[]{:S(2)}) collective-permute-start(bf16[256,512]{1,0:T(8,128)(2,1)S(1)} %add_convert_fusion.4), channel_id=1, source_target_pairs={{0,14},{2,0},{4,2},{6,4},{8,6},{10,8},{12,10},{14,12},{1,15},{3,1}... | collective-permute-start | bytes 786440 | tf_op jit(solution)/shard_map/ppermute | solution.py:132
  68.2 6.7 %collective-permute-start.9 = (bf16[256,512]{1,0:T(8,128)(2,1)S(1)}, bf16[256,512]{1,0:T(8,128)(2,1)S(1)}, u32[]{:S(2)}, u32[]{:S(2)}) collective-permute-start(bf16[256,512]{1,0:T(8,128)(2,1)S(1)} %add_convert_fusion.6), channel_id=1, source_target_pairs={{0,2},{2,4},{4,6},{6,8},{8,10},{10,12},{12,14},{14,0},{1,3},{3,5},... | collective-permute-start | bytes 786440 | tf_op jit(solution)/shard_map/ppermute | solution.py:132
  75.0 4.9 %collective-permute-start.14 = (bf16[128,512]{1,0:T(8,128)(2,1)S(1)}, bf16[128,512]{1,0:T(8,128)(2,1)S(1)}, u32[]{:S(2)}, u32[]{:S(2)}) collective-permute-start(bf16[128,512]{1,0:T(8,128)(2,1)S(1)} %add_convert_fusion.9), channel_id=1, source_target_pairs={{0,1},{1,0},{2,3},{3,2},{4,5},{5,4},{6,7},{7,6},{8,9},{9,8},{10,11... | collective-permute-start | bytes 393224 | tf_op jit(solution)/shard_map/ppermute | solution.py:136
  82.9 21.3 %copy-start.8 = (bf16[128,512]{1,0:T(8,128)(2,1)S(1)}, bf16[128,512]{1,0:T(8,128)(2,1)}, u32[]{:S(2)}) copy-start(bf16[128,512]{1,0:T(8,128)(2,1)} %get-tuple-element.7) | copy-start | bytes 393220
  84.2 6.0 %collective-permute-start.30 = (bf16[256,512]{1,0:T(8,128)(2,1)S(1)}, bf16[256,512]{1,0:T(8,128)(2,1)S(1)}, u32[]{:S(2)}, u32[]{:S(2)}) collective-permute-start(bf16[256,512]{1,0:T(8,128)(2,1)S(1)} %dynamic-slice_convert_fusion), channel_id=1, source_target_pairs={{0,16},{16,0},{32,48},{48,32},{64,80},{80,64},{96,112},{112,96},{1... | collective-permute-start | bytes 786440 | tf_op jit(solution)/shard_map/ppermute | solution.py:223
  90.4 4.8 %collective-permute-start.31 = (bf16[128,512]{1,0:T(8,128)(2,1)S(1)}, bf16[128,512]{1,0:T(8,128)(2,1)S(1)}, u32[]{:S(2)}, u32[]{:S(2)}) collective-permute-start(bf16[128,512]{1,0:T(8,128)(2,1)S(1)} %dynamic-slice_convert_fusion.1), channel_id=1, source_target_pairs={{0,32},{16,48},{32,0},{48,16},{64,96},{80,112},{96,64},{112,80},{1... | collective-permute-start | bytes 393224 | tf_op jit(solution)/shard_map/ppermute | solution.py:223
  95.3 4.7 %collective-permute-start.32 = (bf16[64,512]{1,0:T(8,128)(2,1)S(1)}, bf16[64,512]{1,0:T(8,128)(2,1)S(1)}, u32[]{:S(2)}, u32[]{:S(2)}) collective-permute-start(bf16[64,512]{1,0:T(8,128)(2,1)S(1)} %dynamic-slice_convert_fusion.2), channel_id=1, source_target_pairs={{0,64},{16,80},{32,96},{48,112},{64,0},{80,16},{96,32},{112,48},{1... | collective-permute-start | bytes 196616 | tf_op jit(solution)/shard_map/ppermute | solution.py:223
  100.0 5.4 %collective-permute-start.33 = (bf16[32,512]{1,0:T(8,128)(2,1)S(1)}, bf16[32,512]{1,0:T(8,128)(2,1)S(1)}, u32[]{:S(2)}, u32[]{:S(2)}) collective-permute-start(bf16[32,512]{1,0:T(8,128)(2,1)S(1)} %dynamic-slice_convert_fusion.3), channel_id=1, source_target_pairs={{0,128},{16,144},{32,160},{48,176},{64,192},{80,208},{96,224},{112... | collective-permute-start | bytes 98312 | tf_op jit(solution)/shard_map/ppermute | solution.py:223
  104.2 4.4 %collective-permute-start.15 = (bf16[128,512]{1,0:T(8,128)(2,1)S(1)}, bf16[128,512]{1,0:T(8,128)(2,1)S(1)}, u32[]{:S(2)}, u32[]{:S(2)}) collective-permute-start(bf16[128,512]{1,0:T(8,128)(2,1)S(1)} %copy-done.8), channel_id=1, source_target_pairs={{0,1},{1,0},{2,3},{3,2},{4,5},{5,4},{6,7},{7,6},{8,9},{9,8},{10,11... | collective-permute-start | bytes 393224 | tf_op jit(solution)/shard_map/ppermute | solution.py:136
  105.5 5.8 %collective-permute-start.34 = (bf16[32,512]{1,0:T(8,128)(2,1)S(1)}, bf16[32,512]{1,0:T(8,128)(2,1)S(1)}, u32[]{:S(2)}, u32[]{:S(2)}) collective-permute-start(bf16[32,512]{1,0:T(8,128)(2,1)S(1)} %add_convert_fusion.16), channel_id=1, source_target_pairs={{0,1},{1,0},{2,3},{3,2},{4,5},{5,4},{6,7},{7,6},{8,9},{9,8},{10,11... | collective-permute-start | bytes 98312 | tf_op jit(solution)/shard_map/ppermute | solution.py:136
  108.5 6.5 %collective-permute-start.19 = (bf16[256,512]{1,0:T(8,128)(2,1)S(1)}, bf16[256,512]{1,0:T(8,128)(2,1)S(1)}, u32[]{:S(2)}, u32[]{:S(2)}) collective-permute-start(bf16[256,512]{1,0:T(8,128)(2,1)S(1)} %constant_dynamic-update-slice_fusion.3.refs_1_), channel_id=1, source_target_pairs={{0,2},{2,4},{4,6},{6,8},{8,10},{10,12},{12,14},{14,0},{1,3},{3,5},... | collective-permute-start | bytes 786440 | tf_op jit(solution)/shard_map/ppermute | solution.py:132
  108.6 6.4 %collective-permute-start.16 = (bf16[256,512]{1,0:T(8,128)(2,1)S(1)}, bf16[256,512]{1,0:T(8,128)(2,1)S(1)}, u32[]{:S(2)}, u32[]{:S(2)}) collective-permute-start(bf16[256,512]{1,0:T(8,128)(2,1)S(1)} %constant_dynamic-update-slice_fusion.3.refs_1_), channel_id=1, source_target_pairs={{0,14},{2,0},{4,2},{6,4},{8,6},{10,8},{12,10},{14,12},{1,15},{3,1}... | collective-permute-start | bytes 786440 | tf_op jit(solution)/shard_map/ppermute | solution.py:132
  111.3 6.4 %collective-permute-start.35 = (bf16[32,512]{1,0:T(8,128)(2,1)S(1)}, bf16[32,512]{1,0:T(8,128)(2,1)S(1)}, u32[]{:S(2)}, u32[]{:S(2)}) collective-permute-start(bf16[32,512]{1,0:T(8,128)(2,1)S(1)} %add_convert_fusion.15), channel_id=1, source_target_pairs={{0,2},{2,0},{4,6},{6,4},{8,10},{10,8},{12,14},{14,12},{1,3},{3,1},... | collective-permute-start | bytes 98312 | tf_op jit(solution)/shard_map/ppermute | solution.py:227
  115.0 6.6 %collective-permute-start.20 = (bf16[256,512]{1,0:T(8,128)(2,1)S(1)}, bf16[256,512]{1,0:T(8,128)(2,1)S(1)}, u32[]{:S(2)}, u32[]{:S(2)}) collective-permute-start(bf16[256,512]{1,0:T(8,128)(2,1)S(1)} %collective-permute-done.19.refs_9_), channel_id=1, source_target_pairs={{0,2},{2,4},{4,6},{6,8},{8,10},{10,12},{12,14},{14,0},{1,3},{3,5},... | collective-permute-start | bytes 786440 | tf_op jit(solution)/shard_map/ppermute | solution.py:132
  115.0 6.6 %collective-permute-start.17 = (bf16[256,512]{1,0:T(8,128)(2,1)S(1)}, bf16[256,512]{1,0:T(8,128)(2,1)S(1)}, u32[]{:S(2)}, u32[]{:S(2)}) collective-permute-start(bf16[256,512]{1,0:T(8,128)(2,1)S(1)} %collective-permute-done.16.refs_2_), channel_id=1, source_target_pairs={{0,14},{2,0},{4,2},{6,4},{8,6},{10,8},{12,10},{14,12},{1,15},{3,1}... | collective-permute-start | bytes 786440 | tf_op jit(solution)/shard_map/ppermute | solution.py:132
  117.7 6.9 %collective-permute-start.36 = (bf16[32,512]{1,0:T(8,128)(2,1)S(1)}, bf16[32,512]{1,0:T(8,128)(2,1)S(1)}, u32[]{:S(2)}, u32[]{:S(2)}) collective-permute-start(bf16[32,512]{1,0:T(8,128)(2,1)S(1)} %add_convert_fusion.14), channel_id=1, source_target_pairs={{0,4},{2,6},{4,0},{6,2},{8,12},{10,14},{12,8},{14,10},{1,5},{3,7},... | collective-permute-start | bytes 98312 | tf_op jit(solution)/shard_map/ppermute | solution.py:227
  121.6 16.3 %copy-start.4 = (bf16[256,512]{1,0:T(8,128)(2,1)}, bf16[256,512]{1,0:T(8,128)(2,1)S(1)}, u32[]{:S(2)}) copy-start(bf16[256,512]{1,0:T(8,128)(2,1)S(1)} %collective-permute-done.20.refs_8_) | copy-start | bytes 786436
  121.6 19.6 %collective-permute-start.21 = (bf16[256,512]{1,0:T(8,128)(2,1)S(1)}, bf16[256,512]{1,0:T(8,128)(2,1)S(1)}, u32[]{:S(2)}, u32[]{:S(2)}) collective-permute-start(bf16[256,512]{1,0:T(8,128)(2,1)S(1)} %collective-permute-done.20.refs_8_), channel_id=1, source_target_pairs={{0,2},{2,4},{4,6},{6,8},{8,10},{10,12},{12,14},{14,0},{1,3},{3,5},... | collective-permute-start | bytes 786440 | tf_op jit(solution)/shard_map/ppermute | solution.py:132
  121.6 16.3 %copy-start.6 = (bf16[256,512]{1,0:T(8,128)(2,1)}, bf16[256,512]{1,0:T(8,128)(2,1)S(1)}, u32[]{:S(2)}) copy-start(bf16[256,512]{1,0:T(8,128)(2,1)S(1)} %collective-permute-done.17.refs_3_) | copy-start | bytes 786436
  121.7 19.9 %collective-permute-start.18 = (bf16[256,512]{1,0:T(8,128)(2,1)S(1)}, bf16[256,512]{1,0:T(8,128)(2,1)S(1)}, u32[]{:S(2)}, u32[]{:S(2)}) collective-permute-start(bf16[256,512]{1,0:T(8,128)(2,1)S(1)} %collective-permute-done.17.refs_3_), channel_id=1, source_target_pairs={{0,14},{2,0},{4,2},{6,4},{8,6},{10,8},{12,10},{14,12},{1,15},{3,1}... | collective-permute-start | bytes 786440 | tf_op jit(solution)/shard_map/ppermute | solution.py:132
  124.6 19.7 %collective-permute-start.37 = (bf16[32,512]{1,0:T(8,128)(2,1)S(1)}, bf16[32,512]{1,0:T(8,128)(2,1)S(1)}, u32[]{:S(2)}, u32[]{:S(2)}) collective-permute-start(bf16[32,512]{1,0:T(8,128)(2,1)S(1)} %add_convert_fusion.13), channel_id=1, source_target_pairs={{0,8},{2,10},{4,12},{6,14},{8,0},{10,2},{12,4},{14,6},{1,9},{3,11}... | collective-permute-start | bytes 98312 | tf_op jit(solution)/shard_map/ppermute | solution.py:227
  125.2 2.2 %copy-start.1 = (bf16[128,128,128]{2,1,0:T(8,128)(2,1)S(1)}, bf16[128,128,128]{2,1,0:T(8,128)(2,1)}, u32[]{:S(2)}) copy-start(bf16[128,128,128]{2,1,0:T(8,128)(2,1)} %refs_2_.3) | copy-start | bytes 12582916
  137.9 3.3 %copy-start.2 = (bf16[2048,2048]{1,0:T(8,128)(2,1)}, bf16[2048,2048]{1,0:T(8,128)(2,1)S(1)}, u32[]{:S(2)}) copy-start(bf16[2048,2048]{1,0:T(8,128)(2,1)S(1)} %flipped_build.1.refs_0_) | copy-start | bytes 25165828
  141.3 5.3 %collective-permute-start.22 = (bf16[128,512]{1,0:T(8,128)(2,1)S(1)}, bf16[128,512]{1,0:T(8,128)(2,1)S(1)}, u32[]{:S(2)}, u32[]{:S(2)}) collective-permute-start(bf16[128,512]{1,0:T(8,128)(2,1)S(1)} %slice.170), channel_id=1, source_target_pairs={{0,2},{2,4},{4,6},{6,8},{8,10},{10,12},{12,14},{14,0},{1,3},{3,5},... | collective-permute-start | bytes 393224 | tf_op jit(solution)/shard_map/ppermute | solution.py:132
  141.6 5.0 %collective-permute-start.23 = (bf16[128,512]{1,0:T(8,128)(2,1)S(1)}, bf16[128,512]{1,0:T(8,128)(2,1)S(1)}, u32[]{:S(2)}, u32[]{:S(2)}) collective-permute-start(bf16[128,512]{1,0:T(8,128)(2,1)S(1)} %slice.171), channel_id=1, source_target_pairs={{0,14},{2,0},{4,2},{6,4},{8,6},{10,8},{12,10},{14,12},{1,15},{3,1}... | collective-permute-start | bytes 393224 | tf_op jit(solution)/shard_map/ppermute | solution.py:132
  144.4 18.7 %collective-permute-start.38 = (bf16[32,512]{1,0:T(8,128)(2,1)S(1)}, bf16[32,512]{1,0:T(8,128)(2,1)S(1)}, u32[]{:S(2)}, u32[]{:S(2)}) collective-permute-start(bf16[32,512]{1,0:T(8,128)(2,1)S(1)} %add_convert_fusion.12), channel_id=1, source_target_pairs={{0,128},{16,144},{32,160},{48,176},{64,192},{80,208},{96,224},{112... | collective-permute-start | bytes 98312 | tf_op jit(solution)/shard_map/ppermute | solution.py:223
  146.6 3.4 %copy-start.3 = (bf16[2048,2048]{1,0:T(8,128)(2,1)S(1)}, bf16[2048,2048]{1,0:T(8,128)(2,1)}, u32[]{:S(2)}) copy-start(bf16[2048,2048]{1,0:T(8,128)(2,1)} %copy-done.2) | copy-start | bytes 25165828
  150.0 0.9 copy-start.5
  150.9 0.9 copy-start.7
  158.1 9.1 %collective-permute-start.25 = (bf16[256,512]{1,0:T(8,128)(2,1)S(1)}, bf16[256,512]{1,0:T(8,128)(2,1)S(1)}, u32[]{:S(2)}, u32[]{:S(2)}) collective-permute-start(bf16[256,512]{1,0:T(8,128)(2,1)S(1)} %slice.177), channel_id=1, source_target_pairs={{0,16},{16,0},{32,48},{48,32},{64,80},{80,64},{96,112},{112,96},{1... | collective-permute-start | bytes 786440 | tf_op jit(solution)/shard_map/ppermute | solution.py:115
  163.1 6.3 %collective-permute-start.24 = (bf16[512,512]{1,0:T(8,128)(2,1)S(1)}, bf16[512,512]{1,0:T(8,128)(2,1)S(1)}, u32[]{:S(2)}, u32[]{:S(2)}) collective-permute-start(bf16[512,512]{1,0:T(8,128)(2,1)S(1)} %slice.174), channel_id=1, source_target_pairs={{0,16},{16,0},{32,48},{48,32},{64,80},{80,64},{96,112},{112,96},{1... | collective-permute-start | bytes 1572872 | tf_op jit(solution)/shard_map/ppermute | solution.py:115
  163.2 6.2 %collective-permute-start.39 = (bf16[64,512]{1,0:T(8,128)(2,1)S(1)}, bf16[64,512]{1,0:T(8,128)(2,1)S(1)}, u32[]{:S(2)}, u32[]{:S(2)}) collective-permute-start(bf16[64,512]{1,0:T(8,128)(2,1)S(1)} %pad_maximum_fusion.6), channel_id=1, source_target_pairs={{0,64},{16,80},{32,96},{48,112},{64,0},{80,16},{96,32},{112,48},{1... | collective-permute-start | bytes 196616 | tf_op jit(solution)/shard_map/ppermute | solution.py:223
  168.0 6.7 %collective-permute-start.26 = (bf16[256,512]{1,0:T(8,128)(2,1)}, bf16[256,512]{1,0:T(8,128)(2,1)}, u32[]{:S(2)}, u32[]{:S(2)}) collective-permute-start(bf16[256,512]{1,0:T(8,128)(2,1)} %add_convert_fusion.3), channel_id=1, source_target_pairs={{0,96},{16,48},{32,0},{48,80},{64,32},{80,112},{96,64},{112,16},{1... | collective-permute-start | bytes 786440 | tf_op jit(solution)/shard_map/ppermute | solution.py:128
  176.0 11.9 %collective-permute-start.27 = (bf16[512,512]{1,0:T(8,128)(2,1)S(1)}, bf16[512,512]{1,0:T(8,128)(2,1)S(1)}, u32[]{:S(2)}, u32[]{:S(2)}) collective-permute-start(bf16[512,512]{1,0:T(8,128)(2,1)S(1)} %pad_maximum_fusion), channel_id=1, source_target_pairs={{0,96},{16,48},{32,0},{48,80},{64,32},{80,112},{96,64},{112,16},{1... | collective-permute-start | bytes 1572872 | tf_op jit(solution)/shard_map/ppermute | solution.py:128
  176.1 8.9 %collective-permute-start.40 = (bf16[128,512]{1,0:T(8,128)(2,1)S(1)}, bf16[128,512]{1,0:T(8,128)(2,1)S(1)}, u32[]{:S(2)}, u32[]{:S(2)}) collective-permute-start(bf16[128,512]{1,0:T(8,128)(2,1)S(1)} %pad_maximum_fusion.5), channel_id=1, source_target_pairs={{0,32},{16,48},{32,0},{48,16},{64,96},{80,112},{96,64},{112,80},{1... | collective-permute-start | bytes 393224 | tf_op jit(solution)/shard_map/ppermute | solution.py:223
  185.1 4.0 %collective-permute-start.41 = (bf16[256,512]{1,0:T(8,128)(2,1)S(1)}, bf16[256,512]{1,0:T(8,128)(2,1)S(1)}, u32[]{:S(2)}, u32[]{:S(2)}) collective-permute-start(bf16[256,512]{1,0:T(8,128)(2,1)S(1)} %pad_maximum_fusion.4), channel_id=1, source_target_pairs={{0,16},{16,0},{32,48},{48,32},{64,80},{80,64},{96,112},{112,96},{1... | collective-permute-start | bytes 786440 | tf_op jit(solution)/shard_map/ppermute | solution.py:223
  188.0 1.6 collective-permute-start.28
  189.6 6.5 %collective-permute-start.29 = (bf16[128,512]{1,0:T(8,128)(2,1)S(1)}, bf16[128,512]{1,0:T(8,128)(2,1)S(1)}, u32[]{:S(2)}, u32[]{:S(2)}) collective-permute-start(bf16[128,512]{1,0:T(8,128)(2,1)S(1)} %fusion), channel_id=1, source_target_pairs={{0,128},{16,144},{32,160},{48,176},{64,192},{80,208},{96,224},{112... | collective-permute-start | bytes 393224 | tf_op jit(solution)/shard_map/ppermute | solution.py:119
